TPU v7x, 512 devices: a whole 4x8x8 slice. The times are simulated.
512 devices in a mesh: ctx: 32 (over x, z), head: 16 (over y, core).
Axes of the slice: x: 4, y: 8, z: 8, core: 2. Of those that a mesh axis runs over, the one named last changes fastest.
Arguments:
- queries: bfloat16 [4096, 4096], P('ctx', 'head'), may hold values from -24 to 24
- key_rows: bfloat16 [4096, 4096], P('ctx', 'head'), may hold values from -24 to 24
- value_rows: bfloat16 [4096, 4096], P('ctx', 'head'), may hold values from -6 to 6
- upstream: bfloat16 [4096, 6144], P('ctx', 'head'), may hold values from -6 to 6
- out_weight: bfloat16 [6144, 4096], P('ctx', 'head'), may hold values from -0.078125 to 0.078125
- group_ids: int32 [4096], replicated, may hold values from 0 to 31, never falling along the last dimension, each value on 1 to 256 neighbouring positions
Outputs:
- grad_queries: bfloat16 [4096, 4096], P('ctx', 'head')
- grad_keys: bfloat16 [4096, 4096], P('ctx', 'head')
- grad_values: bfloat16 [4096, 4096], P('ctx', 'head')
Inputs may be any that keep to these rules, and one draw needn't show every extreme that they name: `group_ids`: never falling along the tokens; each group number covers 1 to 256 consecutive tokens, one exactly 256.
All inputs are finite; a program needn't handle non-finite values.
Results may differ from a plain program's by a relative error of at most 0.025.
Values may be sent and summed in bfloat16 or wider, within the bound.
A program may use at most 64 MiB of HBM per device.

v0:
```python
import jax
import jax.numpy as jnp
from jax import lax
from jax.sharding import PartitionSpec as P

HDIM = 128


masked_score = -1e30


def body(queries, key_rows, value_rows, upstream, out_weight, group_ids):
    rows_dev = queries.shape[0]
    heads_dev = queries.shape[1] // HDIM
    scaling = HDIM ** (-0.5)
    own_start = lax.axis_index("ctx") * rows_dev
    own_ids = lax.dynamic_slice_in_dim(group_ids, own_start, rows_dev, 0)
    upstream_full = lax.all_gather(upstream, "head", axis=1, tiled=True)
    grad_out = jnp.dot(
        upstream_full,
        lax.all_gather(out_weight, "ctx", axis=0, tiled=True),
        preferred_element_type=jnp.float32,
    ).astype(jnp.bfloat16)
    query_heads = queries.reshape(rows_dev, heads_dev, HDIM)
    grad_heads = grad_out.reshape(rows_dev, heads_dev, HDIM)
    key_heads = key_rows.reshape(rows_dev, heads_dev, HDIM)
    value_heads = value_rows.reshape(rows_dev, heads_dev, HDIM)
    stats_shape = (heads_dev, rows_dev)
    key_piece = lax.all_gather(key_rows, "ctx", axis=0, tiled=True)
    piece_rows = key_piece.shape[0]
    piece_ids = group_ids
    key_block = key_piece.reshape(piece_rows, heads_dev, HDIM)
    allowed = (piece_ids[None, :] <= own_ids[:, None])[None]
    run_max = jnp.full(stats_shape, masked_score, jnp.float32)
    scores = scaling * jnp.einsum(
        "qhd,khd->hqk", query_heads, key_block, preferred_element_type=jnp.float32
    )
    scores = jnp.where(allowed, scores, masked_score)
    new_max = jnp.maximum(run_max, jnp.max(scores, axis=2))
    weights = jnp.where(allowed, jnp.exp(scores - new_max[:, :, None]), 0.0)
    run_sum = jnp.sum(weights, axis=2)
    run_max, run_sum = (new_max, run_sum)
    log_total = run_max + jnp.log(run_sum)
    key_piece = lax.all_gather(key_rows, "ctx", axis=0, tiled=True)
    value_piece = lax.all_gather(value_rows, "ctx", axis=0, tiled=True)
    piece_rows = key_piece.shape[0]
    piece_ids = group_ids
    key_block = key_piece.reshape(piece_rows, heads_dev, HDIM)
    value_block = value_piece.reshape(piece_rows, heads_dev, HDIM)
    allowed = (piece_ids[None, :] <= own_ids[:, None])[None]
    scores = scaling * jnp.einsum(
        "qhd,khd->hqk", query_heads, key_block, preferred_element_type=jnp.float32
    )
    probs = jnp.where(allowed, jnp.exp(scores - log_total[:, :, None]), 0.0)
    probs_low = probs.astype(jnp.bfloat16)
    grad_probs = jnp.einsum(
        "qhd,khd->hqk", grad_heads, value_block, preferred_element_type=jnp.float32
    )
    mixed_low = (probs * grad_probs).astype(jnp.bfloat16)
    out_acc = jnp.einsum("hqk,khd->hqd", probs_low, value_block, preferred_element_type=jnp.float32)
    mixed_acc = jnp.einsum("hqk,khd->hqd", mixed_low, key_block, preferred_element_type=jnp.float32)
    plain_acc = jnp.einsum("hqk,khd->hqd", probs_low, key_block, preferred_element_type=jnp.float32)
    forward = (out_acc, mixed_acc, plain_acc)
    attn_out, mixed_acc, plain_acc = forward
    delta = jnp.einsum("qhd,hqd->hq", grad_heads.astype(jnp.float32), attn_out)
    grad_query = scaling * (mixed_acc - delta[:, :, None] * plain_acc)
    grad_queries = (
        grad_query.transpose(1, 0, 2).reshape(rows_dev, heads_dev * HDIM).astype(jnp.bfloat16)
    )
    all_lse, all_delta = (
        lax.all_gather(log_total.T, "ctx", axis=0, tiled=True),
        lax.all_gather(delta.T, "ctx", axis=0, tiled=True),
    )
    query_piece = lax.all_gather(queries, "ctx", axis=0, tiled=True)
    grad_piece = lax.all_gather(grad_out, "ctx", axis=0, tiled=True)
    piece_rows = query_piece.shape[0]
    piece_ids = group_ids
    piece_lse = all_lse.T
    piece_delta = all_delta.T
    query_block = query_piece.reshape(piece_rows, heads_dev, HDIM)
    grad_block = grad_piece.reshape(piece_rows, heads_dev, HDIM)
    allowed = (own_ids[None, :] <= piece_ids[:, None])[None]
    scores = scaling * jnp.einsum(
        "qhd,khd->hqk", query_block, key_heads, preferred_element_type=jnp.float32
    )
    probs = jnp.where(allowed, jnp.exp(scores - piece_lse[:, :, None]), 0.0)
    probs_low = probs.astype(jnp.bfloat16)
    grad_probs = jnp.einsum(
        "qhd,khd->hqk", grad_block, value_heads, preferred_element_type=jnp.float32
    )
    grad_scores = (probs * (grad_probs - piece_delta[:, :, None])).astype(jnp.bfloat16)
    value_grad = jnp.einsum(
        "hqk,qhd->hkd", probs_low, grad_block, preferred_element_type=jnp.float32
    )
    key_grad = jnp.einsum(
        "hqk,qhd->hkd", grad_scores, query_block, preferred_element_type=jnp.float32
    )
    key_grad, value_grad = (key_grad, value_grad)
    grad_keys = (
        (scaling * key_grad)
        .transpose(1, 0, 2)
        .reshape(rows_dev, heads_dev * HDIM)
        .astype(jnp.bfloat16)
    )
    grad_values = (
        value_grad.transpose(1, 0, 2).reshape(rows_dev, heads_dev * HDIM).astype(jnp.bfloat16)
    )
    return (grad_queries, grad_keys, grad_values)


def solution(mesh):
    in_specs = (
        P("ctx", "head"),
        P("ctx", "head"),
        P("ctx", "head"),
        P("ctx", "head"),
        P("ctx", "head"),
        P(),
    )
    out_specs = (P("ctx", "head"), P("ctx", "head"), P("ctx", "head"))
    return jax.shard_map(body, mesh=mesh, in_specs=in_specs, out_specs=out_specs, check_vma=False)
```

profile of v0, /device:TPU:24, one launch (start us, length us, event | category | flops | bytes accessed | tf_op | source)
XLA Modules:
  0.0 497.6 jit_solution(7803111154244521029)
XLA Ops:
  7.2 0.0 copy-start.4
  7.2 0.0 all-gather.9.cloned.1.call-start
  7.2 0.7 all-gather.9.cloned.1.call-update
  7.9 0.0 all-gather.11.cloned.1.call-start
  8.0 0.7 all-gather.11.cloned.1.call-update
  8.7 0.0 all-gather.7.cloned.1.call-start
  8.7 1.6 copy.18
  10.3 0.0 all-gather.7.cloned.1.call-update
  10.3 0.0 copy-start.3
  10.3 0.0 all-gather.15.cloned.1.call-start
  10.4 1.6 copy.21
  12.0 0.0 all-gather.15.cloned.1.call-update
  12.0 0.0 all-gather.13.cloned.1.call-start
  12.0 0.5 all-gather.13.cloned.1.call-update
  12.6 0.0 all-gather.17.cloned.1.call-start
  12.6 1.0 copy.41
  13.6 0.8 dynamic_slice.3
  14.3 1.1 broadcast_compare_fusion.1
  15.4 40.1 %all-gather.9.cloned.1.call-done = bf16[128,6144]{1,0:T(8,128)(2,1)} async-done(((bf16[128,384]{1,0:T(8,128)(2,1)}), bf16[128,6144]{1,0:T(8,128)(2,1)}) %all-gather.9.cloned.1.call-update) | async-done | bytes 1572880 | tf_op jit(solution)/shard_map/all_gather | solution.py:18
  55.5 88.5 %all-gather.11.cloned.1.call-done = bf16[6144,256]{1,0:T(8,128)(2,1)} async-done(((bf16[192,256]{1,0:T(8,128)(2,1)}), bf16[6144,256]{1,0:T(8,128)(2,1)}) %all-gather.11.cloned.1.call-update) | async-done | bytes 3145744 | tf_op jit(solution)/shard_map/all_gather | solution.py:21
  144.0 3.6 convolution_convert_fusion
  147.6 0.0 all-gather.17.cloned.1.call-update
  147.6 0.0 copy-done.4
  147.6 1.9 broadcast_compare_fusion
  149.5 75.5 %all-gather.7.cloned.1.call-done = bf16[4096,256]{0,1:T(8,128)(2,1)} async-done(((bf16[128,256]{0,1:T(8,128)(2,1)}), bf16[4096,256]{0,1:T(8,128)(2,1)}) %all-gather.7.cloned.1.call-update) | async-done | bytes 2097168 | tf_op jit(solution)/shard_map/all_gather | solution.py:44
  225.0 0.0 copy-done.3
  225.0 2.8 select_reduce_fusion.1
  227.8 0.0 copy-start.5
  227.8 2.0 copy-done
  229.8 1.2 select_reduce_fusion
  231.0 42.6 %all_gather.30 = f32[4096,2]{0,1:T(2,128)S(1)} all-gather(f32[128,2]{0,1:T(2,128)S(1)} %bitcast.95), channel_id=1, replica_groups=mesh['ctx'=32,'head'=16] {'ctx'}, dimensions={0}, use_global_device_ids=true | all-gather | bytes 33792 | tf_op jit(solution)/shard_map/all_gather | solution.py:71
  273.6 34.8 %all-gather.15.cloned.1.call-done = bf16[4096,256]{0,1:T(8,128)(2,1)} async-done(((bf16[128,256]{0,1:T(8,128)(2,1)}), bf16[4096,256]{0,1:T(8,128)(2,1)}) %all-gather.15.cloned.1.call-update) | async-done | bytes 2097168 | tf_op jit(solution)/shard_map/all_gather | solution.py:74
  308.4 0.0 copy-done.5
  308.4 4.5 fusion.3
  313.0 81.3 %all-gather.13.cloned.1.call-done = bf16[4096,256]{1,0:T(8,128)(2,1)} async-done(((bf16[128,256]{1,0:T(8,128)(2,1)}), bf16[4096,256]{1,0:T(8,128)(2,1)}) %all-gather.13.cloned.1.call-update) | async-done | bytes 2097168 | tf_op jit(solution)/shard_map/all_gather | solution.py:45
  394.2 4.0 fusion.22
  398.2 0.2 multiply_reduce_fusion
  398.5 0.1 copy.37
  398.5 4.7 fusion.19
  403.2 3.2 fusion.28
  406.4 0.7 copy.25
  407.1 41.5 %all_gather.32 = f32[4096,2]{0,1:T(2,128)S(1)} all-gather(f32[128,2]{0,1:T(2,128)S(1)} %copy.37), channel_id=1, replica_groups=mesh['ctx'=32,'head'=16] {'ctx'}, dimensions={0}, use_global_device_ids=true | all-gather | bytes 33792 | tf_op jit(solution)/shard_map/all_gather | solution.py:72
  448.7 30.0 %all-gather.17.cloned.1.call-done = bf16[4096,256]{1,0:T(8,128)(2,1)} async-done(((bf16[128,256]{1,0:T(8,128)(2,1)}), bf16[4096,256]{1,0:T(8,128)(2,1)}) %all-gather.17.cloned.1.call-update) | async-done | bytes 2097168 | tf_op jit(solution)/shard_map/all_gather | solution.py:75
  478.7 2.9 copy.42
  481.6 2.9 fusion.30
  484.5 4.8 fusion.29
  489.3 0.7 copy.26
  490.0 0.7 copy.27
  (8 shorter events, 0.0 us)
Async XLA Ops:
  7.2 140.4 %copy-start.4 = (s32[4096]{0:T(1024)S(1)}, s32[4096]{0:T(1024)}, u32[]{:S(2)}) copy-start(s32[4096]{0:T(1024)} %param.11) | copy-start | bytes 49156
  7.2 48.4 %all-gather.9.cloned.1.call-start = ((), (), s32[]{:S(2)}) async-start(), calls=%async_computation.1 | async-start | bytes 1671168 | tf_op jit(solution)/shard_map/all_gather | solution.py:18
  7.9 136.1 %all-gather.11.cloned.1.call-start = ((), (), s32[]{:S(2)}) async-start(), calls=%async_computation.2 | async-start | bytes 3244032 | tf_op jit(solution)/shard_map/all_gather | solution.py:21
  8.7 216.4 %all-gather.7.cloned.1.call-start = ((), (), s32[]{:S(2)}) async-start(), calls=%async_computation | async-start | bytes 2162688 | tf_op jit(solution)/shard_map/all_gather | solution.py:44
  10.3 214.7 %copy-start.3 = (bf16[128,256]{1,0:T(8,128)(2,1)S(1)}, bf16[128,256]{1,0:T(8,128)(2,1)}, u32[]{:S(2)}) copy-start(bf16[128,256]{1,0:T(8,128)(2,1)} %param.6) | copy-start | bytes 196612
  10.3 298.1 %all-gather.15.cloned.1.call-start = ((), (), s32[]{:S(2)}) async-start(), calls=%async_computation.4 | async-start | bytes 2162688 | tf_op jit(solution)/shard_map/all_gather | solution.py:74
  12.0 382.2 %all-gather.13.cloned.1.call-start = ((), (), s32[]{:S(2)}) async-start(), calls=%async_computation.3 | async-start | bytes 2162688 | tf_op jit(solution)/shard_map/all_gather | solution.py:45
  12.6 466.1 %all-gather.17.cloned.1.call-start = ((), (), s32[]{:S(2)}) async-start(), calls=%async_computation.5 | async-start | bytes 2162688 | tf_op jit(solution)/shard_map/all_gather | solution.py:75
  227.8 2.0 copy-start
  227.8 80.6 %copy-start.5 = (bf16[128,256]{1,0:T(8,128)(2,1)S(1)}, bf16[128,256]{1,0:T(8,128)(2,1)}, u32[]{:S(2)}) copy-start(bf16[128,256]{1,0:T(8,128)(2,1)} %param.7) | copy-start | bytes 196612
  313.0 85.2 %copy-start.2 = (bf16[128,256]{1,0:T(8,128)(2,1)S(1)}, bf16[128,256]{1,0:T(8,128)(2,1)}, u32[]{:S(2)}) copy-start(bf16[128,256]{1,0:T(8,128)(2,1)} %convolution_convert_fusion) | copy-start | bytes 196612
  313.0 85.6 %copy-start.1 = (bf16[4096,256]{0,1:T(8,128)(2,1)S(1)}, bf16[4096,256]{0,1:T(8,128)(2,1)}, u32[]{:S(2)}) copy-start(bf16[4096,256]{0,1:T(8,128)(2,1)} %all-gather.7.cloned.1.call-done) | copy-start | bytes 6291460
Sparse Core Ops, SparseCore 0:
  10.1 45.4 all-gather.8
  58.7 85.2 all-gather.10
  147.6 77.3 all-gather.6
  228.5 79.9 all-gather.14
  311.5 82.7 all-gather.12
  397.8 80.7 all-gather.16
where the time goes:
time: 498 us
  waiting for transfers between devices  352 us (71%)
  blocking collectives  84.1 us (17%)
  matrix products  30.4 us (6%)
  between operations  14.2 us (3%)
  local copies, waits for them, and re-layouts  12.1 us (2%)
    all_gather x1, waiting for transfers between devices, body(): lax.all_gather(out_weight, 'ctx', axis=0, tiled=True)  88.5 us
    all_gather x1, waiting for transfers between devices, body(): value_piece = lax.all_gather(value_rows, 'ctx', axis=0, tiled=True)  81.3 us
    all_gather x1, waiting for transfers between devices, body(): key_piece = lax.all_gather(key_rows, 'ctx', axis=0, tiled=True)  75.5 us
    all_gather x1, blocking collectives, body(): lax.all_gather(log_total.T, 'ctx', axis=0, tiled=True)  42.6 us
    all_gather x1, blocking collectives, body(): lax.all_gather(delta.T, 'ctx', axis=0, tiled=True)  41.5 us
    all_gather x1, waiting for transfers between devices, body(): upstream_full = lax.all_gather(upstream, 'head', axis=1, tiled=True)  40.1 us
    all_gather x1, waiting for transfers between devices, body(): query_piece = lax.all_gather(queries, 'ctx', axis=0, tiled=True)  34.8 us
    all_gather x1, waiting for transfers between devices, body(): grad_piece = lax.all_gather(grad_out, 'ctx', axis=0, tiled=True)  30 us
  transfers between devices with their start and end apart: 6, of which 6 were waited for; matrix products, arithmetic and copies ran while one was open for 7% of the time, Pallas kernels for 0%

commit v1 on v0

v1 whole, which is shorter than its diff:
```python
import functools

import jax
import jax.numpy as jnp
from jax import lax
from jax.experimental import pallas as pl
from jax.experimental.pallas import tpu as pltpu
from jax.sharding import PartitionSpec as P

MESH = pl.DeviceIdType.MESH
HDIM = 128
LOG2E = 1.4426950408889634
MASKED = -1e30
FLOOR = -1e29
F32 = jnp.float32
BF16 = jnp.bfloat16


def kernel(
    X, Z, Y,
    gid, q, k, v, up, w,
    dq_out, dk_out, dv_out,
    ubuf, upx, wbuf, qbuf, kbuf, vbuf, acc, dsend, drecv, dobuf,
    ml_send, ml_recv, u_send, u_recv, kid, kt, p_s, dp_s, kpart, vpart,
    dqsend, dqrecv, dqacc, rsend, rrecv,
    us, ur, ws, wr, kvs, kvr, qs, qr, xs, xr, sbs, sbr,
    ds, dr_, os_, or_, ms, mr, es, er, gs, gr, rs, rr,
):
    K2 = Y // X
    WB = X * Z // (2 * Y)
    R = q.shape[0]
    Q = X * R
    i, j = lax.axis_index("ctx"), lax.axis_index("head")
    x, z = lax.div(i, Z), lax.rem(i, Z)
    y, c = lax.div(j, 2), lax.rem(j, 2)

    def dev(xx, zz, yy, cc):
        return (xx * Z + zz, yy * 2 + cc)

    def add(a, b, n):
        return lax.rem(a + b + n, n)

    def remote(src, dst, s_sem, r_sem, device):
        return pltpu.make_async_remote_copy(
            src_ref=src, dst_ref=dst, send_sem=s_sem, recv_sem=r_sem,
            device_id=device, device_id_type=MESH,
        )

    z_dev = (dev(x, add(z, 1, Z), y, c), dev(x, add(z, -1, Z), y, c))
    y_dev = (dev(x, z, add(y, 1, Y), c), dev(x, z, add(y, -1, Y), c))
    x_dev = [None] + [dev(add(x, d, X), z, y, c) for d in range(1, X)]
    x_src = [add(x, -d, X) for d in range(X)]
    sibling = dev(x, z, y, 1 - c)

    barrier = pltpu.get_barrier_semaphore()
    peers = [*z_dev, *y_dev, *x_dev[1:], sibling]
    for peer in peers:
        pl.semaphore_signal(barrier, inc=1, device_id=peer, device_id_type=MESH)
    pl.semaphore_wait(barrier, len(peers))

    pending = []

    class Ring:
        def __init__(self, n, me, devs, own, buf, s_sem, r_sem):
            self.n, self.me, self.devs = n, me, devs
            self.own, self.buf, self.s, self.r = own, buf, s_sem, r_sem
            self.last = n // 2 - 1

        def chunks(self, d, s):
            return (d,) if s == self.last else (d, 1 - d)

        def block(self, d, s):
            return add(self.me, -s if d == 0 else s, self.n)

        def send(self, d, s, h):
            b = self.block(d, s)
            src = self.own(h) if s == 0 else self.buf(b, h)
            copy = remote(
                src, self.buf(b, h), self.s.at[d, s, h], self.r.at[d, s, h], self.devs[d]
            )
            copy.start()
            pending.append(copy)

        def begin(self):
            for n in range(2):
                for d in range(2):
                    if n < len(self.chunks(d, 0)):
                        self.send(d, 0, self.chunks(d, 0)[n])

        def step(self, s):
            for n in range(2):
                for d in range(2):
                    if n < len(self.chunks(d, s)):
                        h = self.chunks(d, s)[n]
                        b = self.block(d, s + 1)
                        remote(
                            self.buf(b, h), self.buf(b, h), self.s.at[d, s, h],
                            self.r.at[d, s, h], self.devs[d],
                        ).wait_recv()
                        if s < self.last and h in self.chunks(d, s + 1):
                            self.send(d, s + 1, h)

    uh, wh = up.shape[0] // 2, w.shape[0] // 2
    ring_u = Ring(
        Y, y, y_dev,
        lambda h: up.at[pl.ds(h * uh, uh)],
        lambda b, h: ubuf.at[b, pl.ds(h * uh, uh)],
        us, ur,
    )
    ring_w = Ring(
        Z, z, z_dev,
        lambda h: w.at[pl.ds(h * wh, wh)],
        lambda b, h: wbuf.at[b, pl.ds(h * wh, wh)],
        ws, wr,
    )
    ring_kv = Ring(
        Z, z, z_dev,
        lambda h: (k, v)[h],
        lambda b, h: (kbuf, vbuf)[h].at[b],
        kvs, kvr,
    )

    relayed = []

    def relay(block, src, n):
        xt, kk = lax.div(block, K2), lax.rem(block, K2)
        d = add(xt, -x, X)

        def copy():
            return remote(
                src, upx.at[kk, c, x], xs.at[n], xr.at[d, kk], dev(xt, z, y, c)
            )

        @pl.when(d != 0)
        def _():
            copy().start()

        @pl.when(d == 0)
        def _():
            pltpu.make_async_copy(src, upx.at[kk, c, x], xr.at[d, kk]).start()

        relayed.append((d, copy))

    def exchange(src, dst, s_sem, r_sem):
        for d in range(1, X):
            copy = remote(src(add(x, d, X)), dst.at[x], s_sem.at[d], r_sem.at[d], x_dev[d])
            copy.start()
            pending.append(copy)

    def arrive(dst, s_sem, r_sem, d):
        ref = dst.at[x_src[d]]
        remote(ref, ref, s_sem.at[d], r_sem.at[d], x_dev[d]).wait_recv()

    ring_u.begin()
    ring_w.begin()
    relay(y, up, 0)
    exchange(lambda _: q, qbuf, qs, qr)
    wbuf[z] = w[...]
    kbuf[z] = k[...]
    vbuf[z] = v[...]
    qbuf[x] = q[...]
    kv_next = 0
    steps = max(Y, Z) // 2
    for s in range(steps):
        if s < Y // 2:
            ring_u.step(s)
            relay(ring_u.block(0, s + 1), ubuf.at[ring_u.block(0, s + 1)], 2 * s + 1)
            if s < Y // 2 - 1:
                relay(ring_u.block(1, s + 1), ubuf.at[ring_u.block(1, s + 1)], 2 * s + 2)
        if s < Z // 2:
            ring_w.step(s)
        if s == 0:
            ring_kv.begin()
        if s >= 2:
            ring_kv.step(kv_next)
            kv_next += 1

    for b in range(Z):
        row = gid[pl.ds(x * Z + b, 1), :].astype(F32)
        kid[b] = jnp.broadcast_to(row, (R, R)).T
    qid = jnp.concatenate([gid[pl.ds(b * Z + z, 1), :].astype(F32) for b in range(X)], axis=1)

    turn = lax.rem(y - K2 * x + Y * K2, Y)
    near = jnp.where((turn >= 1) & (turn <= Y // 2), 1, 0) if K2 > 1 else 0
    order = [near, 1 - near] if K2 == 2 else list(range(K2))

    def shared(n, kk):
        return remote(upx.at[kk, c], upx.at[kk, c], sbs.at[n], sbr.at[n], sibling)

    for n, kk in enumerate(order):
        for d in range(X):
            dst = upx.at[kk, c, x_src[d]]
            remote(dst, dst, xs.at[0], xr.at[d, kk], sibling).wait_recv()
        copy = shared(n, kk)
        copy.start()
        pending.append(copy)
    for n, kk in enumerate(order):
        shared(n, kk).wait_recv()
        total = None
        for cc in range(2):
            rows = upx[kk, cc].reshape(Q, upx.shape[4])
            weights = wbuf[pl.ds((kk * 2 + cc) * WB, WB)].reshape(upx.shape[4], w.shape[1])
            part = jnp.dot(rows, weights, preferred_element_type=F32)
            total = part if total is None else total + part
        total = total.reshape(acc.shape)
        if n > 0:
            total = total + acc[...]
        if n < K2 - 1:
            acc[...] = total
        else:
            acc[...] = total
            dsend[...] = total.astype(BF16)
    exchange(lambda t: dsend.at[t], drecv, ds, dr_)
    while kv_next < Z // 2 - 1:
        ring_kv.step(kv_next)
        kv_next += 1
    total = acc[x]
    for d in range(1, X):
        arrive(drecv, ds, dr_, d)
        total = total + drecv[x_src[d]].astype(F32)
    dobuf[x] = total.astype(BF16)
    exchange(lambda _: dobuf.at[x], dobuf, os_, or_)
    if kv_next < Z // 2:
        ring_kv.step(kv_next)
    for d in range(1, X):
        arrive(qbuf, qs, qr, d)

    NT = (((1,), (1,)), ((), ()))
    scale = HDIM ** (-0.5)
    cols = [slice(h * HDIM, (h + 1) * HDIM) for h in range(2)]

    def fold(block, op):
        return op(block.reshape(R // 8, 8, Q), axis=0)

    def loop_scores(b, maxima):
        allowed = jnp.tile(kid[b], (1, X)) <= qid
        out = []
        for h in range(2):
            queries = qbuf[:, :, cols[h]].reshape(Q, HDIM)
            s = lax.dot_general(kbuf[b, :, cols[h]], queries, NT, preferred_element_type=F32)
            s = jnp.where(allowed, s * (scale * LOG2E), MASKED)
            p_s[h, b] = s
            kt[b, cols[h], :] = kbuf[b, :, cols[h]].T
            out.append(jnp.maximum(maxima[h], fold(s, jnp.max)))
        return tuple(out)

    start = jnp.full((8, Q), FLOOR, F32)
    maxima = lax.fori_loop(0, Z, loop_scores, (start, start))
    m_own = [jnp.max(m, axis=0, keepdims=True) for m in maxima]

    def loop_exp(b, sums):
        out = []
        for h in range(2):
            e = jnp.exp2(p_s[h, b] - m_own[h])
            p_s[h, b] = e
            out.append(sums[h] + fold(e, jnp.sum))
        return tuple(out)

    zero = jnp.zeros((8, Q), F32)
    sums = lax.fori_loop(0, Z, loop_exp, (zero, zero))
    l_own = [jnp.sum(s, axis=0, keepdims=True) for s in sums]
    ml_send[...] = jnp.concatenate([*m_own, *l_own, jnp.zeros((4, Q), F32)], axis=0)
    exchange(lambda _: ml_send, ml_recv, ms, mr)
    stats = [ml_send[...]]
    for d in range(1, X):
        arrive(ml_recv, ms, mr, d)
        stats.append(ml_recv[x_src[d]])
    factor = []
    for h in range(2):
        m_all = functools.reduce(jnp.maximum, [s[h : h + 1] for s in stats])
        l_all = sum(s[2 + h : 3 + h] * jnp.exp2(s[h : h + 1] - m_all) for s in stats)
        factor.append(jnp.exp2(m_own[h] - m_all) / l_all)

    for d in range(1, X):
        arrive(dobuf, os_, or_, d)

    def loop_probs(b, sums):
        out = []
        for h in range(2):
            grads = dobuf[:, :, cols[h]].reshape(Q, HDIM)
            g = lax.dot_general(vbuf[b, :, cols[h]], grads, NT, preferred_element_type=F32)
            prob = p_s[h, b] * factor[h]
            p_s[h, b] = prob
            dp_s[h, b] = g
            vpart[b, h] = jnp.dot(prob.astype(BF16), grads, preferred_element_type=F32)
            out.append(sums[h] + fold(prob * g, jnp.sum))
        return tuple(out)

    sums = lax.fori_loop(0, Z, loop_probs, (zero, zero))
    u_own = [jnp.sum(s, axis=0, keepdims=True) for s in sums]
    u_send[...] = jnp.concatenate([*u_own, jnp.zeros((6, Q), F32)], axis=0)
    exchange(lambda _: u_send, u_recv, es, er)

    half = Z // 2
    parts = (vpart, kpart)
    factors = (1.0, scale)

    def rs_heads(d, t):
        return (d,) if t == 0 else (0, 1)

    def rs_copy(a, d, t):
        if t == 0:
            src, dst = rsend.at[a, d, t, d], rrecv.at[a, d, t, d]
        else:
            src, dst = rsend.at[a, d, t], rrecv.at[a, d, t]
        return remote(src, dst, rs.at[a, d, t], rr.at[a, d, t], z_dev[d])

    def rs_step(a, t):
        for d in range(2):
            target = add(z, (half - t) if d == 0 else (t - half), Z)
            if t > 0:
                rs_copy(a, d, t - 1).wait_recv()
            for h in rs_heads(d, t):
                value = parts[a][target, h] * factors[a]
                if t > 0 and h in rs_heads(d, t - 1):
                    value = value + rrecv[a, d, t - 1, h].astype(F32)
                rsend[a, d, t, h] = value.astype(BF16)
            copy = rs_copy(a, d, t)
            copy.start()
            pending.append(copy)

    def rs_end(a, out):
        for d in range(2):
            rs_copy(a, d, half - 1).wait_recv()
        for h in range(2):
            value = parts[a][z, h] * factors[a]
            for d in range(2):
                if h in rs_heads(d, half - 1):
                    value = value + rrecv[a, d, half - 1, h].astype(F32)
            out[:, cols[h]] = value.astype(BF16)

    rs_step(0, 0)
    rs_v = 1
    deltas = u_send[...]
    for d in range(1, X):
        arrive(u_recv, es, er, d)
        deltas = deltas + u_recv[x_src[d]]
    delta = [deltas[h : h + 1] for h in range(2)]
    dqacc[...] = jnp.zeros_like(dqacc)

    def loop_grads(b, _):
        for h in range(2):
            g = (p_s[h, b] * (dp_s[h, b] - delta[h])).astype(BF16)
            queries = qbuf[:, :, cols[h]].reshape(Q, HDIM)
            kpart[b, h] = jnp.dot(g, queries, preferred_element_type=F32)
            dqacc[h] += jnp.dot(kt[b, cols[h], :], g, preferred_element_type=F32)
        return 0

    lax.fori_loop(0, Z, loop_grads, 0)
    rs_step(1, 0)
    for b in range(X):
        for h in range(2):
            part = dqacc[h, :, b * R : (b + 1) * R].T * scale
            acc[b, :, cols[h]] = part
            dqsend[b, :, cols[h]] = part.astype(BF16)
    exchange(lambda t: dqsend.at[t], dqrecv, gs, gr)
    for t in range(1, half):
        rs_step(0, t)
        rs_step(1, t)
    total = acc[x]
    for d in range(1, X):
        arrive(dqrecv, gs, gr, d)
        total = total + dqrecv[x_src[d]].astype(F32)
    dq_out[...] = total.astype(BF16)
    rs_end(0, dv_out)
    rs_end(1, dk_out)

    for copy in pending:
        copy.wait_send()
    for d, copy in relayed:

        @pl.when(d != 0)
        def _():
            copy().wait_send()


def body(X, Z, Y, queries, key_rows, value_rows, upstream, out_weight, group_ids):
    R, C = queries.shape
    U = upstream.shape[1]
    W = out_weight.shape[0]
    K2 = Y // X
    Q = X * R
    groups = group_ids.reshape(X * Z, R)
    vmem = pl.BlockSpec(memory_space=pltpu.VMEM)
    dma = pltpu.SemaphoreType.DMA
    V = pltpu.VMEM
    out = jax.ShapeDtypeStruct((R, C), BF16)
    scratch = [
        V((Y, R, U), BF16), V((K2, 2, X, R, U), BF16), V((Z, W, C), BF16), V((X, R, C), BF16),
        V((Z, R, C), BF16), V((Z, R, C), BF16), V((X, R, C), F32), V((X, R, C), BF16),
        V((X, R, C), BF16), V((X, R, C), BF16),
        V((8, Q), F32), V((X, 8, Q), F32), V((8, Q), F32), V((X, 8, Q), F32),
        V((Z, R, R), F32), V((Z, C, R), BF16), V((2, Z, R, Q), F32), V((2, Z, R, Q), F32),
        V((Z, 2, R, HDIM), F32), V((Z, 2, R, HDIM), F32),
        V((X, R, C), BF16), V((X, R, C), BF16), V((2, HDIM, Q), F32),
        V((2, 2, Z // 2, 2, R, HDIM), BF16), V((2, 2, Z // 2, 2, R, HDIM), BF16),
        dma((2, Y // 2, 2)), dma((2, Y // 2, 2)), dma((2, Z // 2, 2)), dma((2, Z // 2, 2)),
        dma((2, Z // 2, 2)), dma((2, Z // 2, 2)), dma((X,)), dma((X,)), dma((Y,)), dma((X, K2)),
        dma((K2,)), dma((K2,)),
        dma((X,)), dma((X,)), dma((X,)), dma((X,)), dma((X,)), dma((X,)), dma((X,)), dma((X,)),
        dma((X,)), dma((X,)), dma((2, 2, Z // 2)), dma((2, 2, Z // 2)),
    ]
    return pl.pallas_call(
        functools.partial(kernel, X, Z, Y),
        out_shape=(out, out, out),
        in_specs=[vmem] * 6,
        out_specs=(vmem, vmem, vmem),
        scratch_shapes=scratch,
        name="attention_backward",
        compiler_params=pltpu.CompilerParams(
            collective_id=0, has_side_effects=True, vmem_limit_bytes=48 * 2**20
        ),
    )(groups, queries, key_rows, value_rows, upstream, out_weight)


def solution(mesh):
    split = P("ctx", "head")
    X, Z, Y = 4, mesh.shape["ctx"] // 4, mesh.shape["head"] // 2
    return jax.shard_map(
        functools.partial(body, X, Z, Y),
        mesh=mesh,
        in_specs=(split, split, split, split, split, P()),
        out_specs=(split, split, split),
        check_vma=False,
    )
```

time: 498 us -> 77.5 us (0.16)
  waiting for transfers between devices: 352 us -> 0 us
  blocking collectives: 84.1 us -> 0 us
  Pallas kernels: 0 us -> 69.6 us
  matrix products: 30.4 us -> 0 us
  between operations: 14.2 us -> 0.65 us
  local copies, waits for them, and re-layouts: 12.1 us -> 6.9 us
    all_gather x6 -> x0, waiting for transfers between devices: 350 us -> none  [the longest x1 88.5 us: body(): lax.all_gather(out_weight, 'ctx', axis=0, tiled=True)]
    all_gather x2 -> x0, blocking collectives: 84.1 us -> none  [the longest x1 42.6 us: body(): lax.all_gather(log_total.T, 'ctx', axis=0, tiled=True)]
    pallas_call x0 -> x1, Pallas kernels: none -> 69.6 us  [body(): pl.pallas_call(functools.partial(kernel, X, Z, Y), out_shape=(out, out, o...]
    dot_general x8 -> x0, matrix products: 30.4 us -> none  [the longest x1 4.79 us: body(): jnp.einsum('hqk,qhd->hkd', grad_scores, query_block, preferred_element_ty...]
  transfers between devices with their start and end apart: 6 -> 0, of which waited for: 6 -> 0; matrix products, arithmetic and copies ran while one was open for 7% -> 0% of each run, Pallas kernels for 0% -> 0%
where the time goes in v1:
time: 77.5 us; the launch traced here: 77.2 us
  Pallas kernels  69.6 us (90%)
  local copies, waits for them, and re-layouts  6.9 us (9%)
    pallas_call x1, Pallas kernels, body(): pl.pallas_call(functools.partial(kernel, X, Z, Y), out_shape=(out, out, o...  69.6 us
    unnamed x15, local copies, waits for them, and re-layouts  6.9 us

profile of v1, /device:TPU:24, one launch (start us, length us, event | category | flops | bytes accessed | tf_op | source)
XLA Modules:
  0.0 77.2 jit_solution(5520904809387971869)
XLA Ops:
  0.6 0.0 copy-start
  0.6 0.9 %copy-done = bf16[128,384]{1,0:T(8,128)(2,1)S(1)} copy-done((bf16[128,384]{1,0:T(8,128)(2,1)S(1)}, bf16[128,384]{1,0:T(8,128)(2,1)}, u32[]{:S(2)}) %copy-start) | copy-done | bytes 98328
  1.5 0.0 copy-start.1
  1.5 0.9 %copy-done.1 = bf16[192,256]{1,0:T(8,128)(2,1)S(1)} copy-done((bf16[192,256]{1,0:T(8,128)(2,1)S(1)}, bf16[192,256]{1,0:T(8,128)(2,1)}, u32[]{:S(2)}) %copy-start.1) | copy-done | bytes 98328
  2.4 0.0 copy-start.2
  2.4 0.8 %copy-done.2 = bf16[128,256]{1,0:T(8,128)(2,1)S(1)} copy-done((bf16[128,256]{1,0:T(8,128)(2,1)S(1)}, bf16[128,256]{1,0:T(8,128)(2,1)}, u32[]{:S(2)}) %copy-start.2) | copy-done | bytes 65560
  3.3 0.0 copy-start.3
  3.3 0.8 %copy-done.3 = bf16[128,256]{1,0:T(8,128)(2,1)S(1)} copy-done((bf16[128,256]{1,0:T(8,128)(2,1)S(1)}, bf16[128,256]{1,0:T(8,128)(2,1)}, u32[]{:S(2)}) %copy-start.3) | copy-done | bytes 65560
  4.1 0.0 copy-start.4
  4.1 0.8 %copy-done.4 = bf16[128,256]{1,0:T(8,128)(2,1)S(1)} copy-done((bf16[128,256]{1,0:T(8,128)(2,1)S(1)}, bf16[128,256]{1,0:T(8,128)(2,1)}, u32[]{:S(2)}) %copy-start.4) | copy-done | bytes 65560
  4.9 0.0 copy-start.5
  4.9 0.7 copy-done.5
  5.7 69.6 %attention_backward.1 = (bf16[128,256]{1,0:T(8,128)(2,1)S(1)}, bf16[128,256]{1,0:T(8,128)(2,1)S(1)}, bf16[128,256]{1,0:T(8,128)(2,1)S(1)}) custom-call(s32[32,128]{1,0:T(8,128)S(1)} %bitcast.1, bf16[128,256]{1,0:T(8,128)(2,1)S(1)} %copy-done.2, bf16[128,256]{1,0:T(8,128)(2,1)S(1)} %copy-done.3, bf16[128,256]{1,0:T(8,128)(2,1)S(1)} %copy-done.4, ...), custom_call_target="tpu_custom_call" | custom-call | tf_op jit(solution)/shard_map/attention_backward/pallas_call | solution.py:403
  75.3 0.6 copy.12
  75.9 0.6 copy.13
  76.5 0.6 copy.14
Async XLA Ops:
  0.6 0.9 %copy-start = (bf16[128,384]{1,0:T(8,128)(2,1)S(1)}, bf16[128,384]{1,0:T(8,128)(2,1)}, u32[]{:S(2)}) copy-start(bf16[128,384]{1,0:T(8,128)(2,1)} %up.1) | copy-start | bytes 294916
  1.5 0.9 %copy-start.1 = (bf16[192,256]{1,0:T(8,128)(2,1)S(1)}, bf16[192,256]{1,0:T(8,128)(2,1)}, u32[]{:S(2)}) copy-start(bf16[192,256]{1,0:T(8,128)(2,1)} %w.1) | copy-start | bytes 294916
  2.4 0.8 %copy-start.2 = (bf16[128,256]{1,0:T(8,128)(2,1)S(1)}, bf16[128,256]{1,0:T(8,128)(2,1)}, u32[]{:S(2)}) copy-start(bf16[128,256]{1,0:T(8,128)(2,1)} %q.1) | copy-start | bytes 196612
  3.3 0.8 %copy-start.3 = (bf16[128,256]{1,0:T(8,128)(2,1)S(1)}, bf16[128,256]{1,0:T(8,128)(2,1)}, u32[]{:S(2)}) copy-start(bf16[128,256]{1,0:T(8,128)(2,1)} %k.1) | copy-start | bytes 196612
  4.1 0.8 %copy-start.4 = (bf16[128,256]{1,0:T(8,128)(2,1)S(1)}, bf16[128,256]{1,0:T(8,128)(2,1)}, u32[]{:S(2)}) copy-start(bf16[128,256]{1,0:T(8,128)(2,1)} %v.1) | copy-start | bytes 196612
  4.9 0.7 copy-start.5

commit v2 on v1

--- a/solution.py
+++ b/solution.py
@@ -12,19 +12,22 @@
 LOG2E = 1.4426950408889634
 MASKED = -1e30
 FLOOR = -1e29
+KV_STEPS = (2, 3)
+NU, NW = 2, 2
 F32 = jnp.float32
 BF16 = jnp.bfloat16
 
 
 def kernel(
     X, Z, Y,
-    gid, q, k, v, up, w,
+    gid_in, q, k, v, up, w,
     dq_out, dk_out, dv_out,
+    gid,
     ubuf, upx, wbuf, qbuf, kbuf, vbuf, acc, dsend, drecv, dobuf,
     ml_send, ml_recv, u_send, u_recv, kid, kt, p_s, dp_s, kpart, vpart,
     dqsend, dqrecv, dqacc, rsend, rrecv,
     us, ur, ws, wr, kvs, kvr, qs, qr, xs, xr, sbs, sbr,
-    ds, dr_, os_, or_, ms, mr, es, er, gs, gr, rs, rr,
+    ds, dr_, os_, or_, ms, mr, es, er, gs, gr, rs, rr, ls,
 ):
     K2 = Y // X
     WB = X * Z // (2 * Y)
@@ -52,70 +55,77 @@
     x_src = [add(x, -d, X) for d in range(X)]
     sibling = dev(x, z, y, 1 - c)
 
+    loads = [
+        pltpu.make_async_copy(src, dst, ls.at[n])
+        for n, (src, dst) in enumerate([
+            (up, ubuf.at[y]), (w, wbuf.at[z]), (k, kbuf.at[z]), (v, vbuf.at[z]),
+            (q, qbuf.at[x]), (gid_in, gid),
+        ])
+    ]
+    for load in loads:
+        load.start()
+
     barrier = pltpu.get_barrier_semaphore()
     peers = [*z_dev, *y_dev, *x_dev[1:], sibling]
     for peer in peers:
         pl.semaphore_signal(barrier, inc=1, device_id=peer, device_id_type=MESH)
     pl.semaphore_wait(barrier, len(peers))
+    for load in loads:
+        load.wait()
 
     pending = []
 
     class Ring:
-        def __init__(self, n, me, devs, own, buf, s_sem, r_sem):
+        def __init__(self, n, me, devs, nc, buf, s_sem, r_sem):
             self.n, self.me, self.devs = n, me, devs
-            self.own, self.buf, self.s, self.r = own, buf, s_sem, r_sem
-            self.last = n // 2 - 1
+            self.buf, self.s, self.r = buf, s_sem, r_sem
+            self.last, self.nc = n // 2 - 1, nc
 
         def chunks(self, d, s):
-            return (d,) if s == self.last else (d, 1 - d)
+            order = list(range(self.nc)) if d == 0 else list(range(self.nc))[::-1]
+            return order[: self.nc // 2] if s == self.last else order
 
         def block(self, d, s):
             return add(self.me, -s if d == 0 else s, self.n)
 
         def send(self, d, s, h):
             b = self.block(d, s)
-            src = self.own(h) if s == 0 else self.buf(b, h)
             copy = remote(
-                src, self.buf(b, h), self.s.at[d, s, h], self.r.at[d, s, h], self.devs[d]
+                self.buf(b, h), self.buf(b, h), self.s.at[d, s, h], self.r.at[d, s, h], self.devs[d]
             )
             copy.start()
             pending.append(copy)
 
-        def begin(self):
-            for n in range(2):
-                for d in range(2):
-                    if n < len(self.chunks(d, 0)):
-                        self.send(d, 0, self.chunks(d, 0)[n])
-
-        def step(self, s):
-            for n in range(2):
-                for d in range(2):
-                    if n < len(self.chunks(d, s)):
-                        h = self.chunks(d, s)[n]
-                        b = self.block(d, s + 1)
-                        remote(
-                            self.buf(b, h), self.buf(b, h), self.s.at[d, s, h],
-                            self.r.at[d, s, h], self.devs[d],
-                        ).wait_recv()
-                        if s < self.last and h in self.chunks(d, s + 1):
-                            self.send(d, s + 1, h)
-
-    uh, wh = up.shape[0] // 2, w.shape[0] // 2
+        def begin(self, n):
+            for d in range(2):
+                if n < len(self.chunks(d, 0)):
+                    self.send(d, 0, self.chunks(d, 0)[n])
+
+        def step(self, s, n):
+            for d in range(2):
+                if n < len(self.chunks(d, s)):
+                    h = self.chunks(d, s)[n]
+                    b = self.block(d, s + 1)
+                    remote(
+                        self.buf(b, h), self.buf(b, h), self.s.at[d, s, h],
+                        self.r.at[d, s, h], self.devs[d],
+                    ).wait_recv()
+                    if s < self.last and h in self.chunks(d, s + 1):
+                        self.send(d, s + 1, h)
+
+    uh, wh = up.shape[0] // NU, w.shape[0] // NW
     ring_u = Ring(
-        Y, y, y_dev,
-        lambda h: up.at[pl.ds(h * uh, uh)],
+        Y, y, y_dev, NU,
         lambda b, h: ubuf.at[b, pl.ds(h * uh, uh)],
         us, ur,
     )
     ring_w = Ring(
-        Z, z, z_dev,
-        lambda h: w.at[pl.ds(h * wh, wh)],
+        Z, z, z_dev, NW,
         lambda b, h: wbuf.at[b, pl.ds(h * wh, wh)],
         ws, wr,
     )
     ring_kv = Ring(
-        Z, z, z_dev,
-        lambda h: (k, v)[h],
+        Z, z, z_dev, 2,
         lambda b, h: (kbuf, vbuf)[h].at[b],
         kvs, kvr,
     )
@@ -151,29 +161,27 @@
         ref = dst.at[x_src[d]]
         remote(ref, ref, s_sem.at[d], r_sem.at[d], x_dev[d]).wait_recv()
 
-    ring_u.begin()
-    ring_w.begin()
-    relay(y, up, 0)
-    exchange(lambda _: q, qbuf, qs, qr)
-    wbuf[z] = w[...]
-    kbuf[z] = k[...]
-    vbuf[z] = v[...]
-    qbuf[x] = q[...]
-    kv_next = 0
-    steps = max(Y, Z) // 2
-    for s in range(steps):
+    for n in range(max(NU, NW)):
+        ring_u.begin(n)
+        ring_w.begin(n)
+    relay(y, ubuf.at[y], 0)
+    exchange(lambda _: qbuf.at[x], qbuf, qs, qr)
+    for s in range(max(Y, Z) // 2):
+        for n in range(max(NU, NW)):
+            if s < Y // 2:
+                ring_u.step(s, n)
+            if s < Z // 2:
+                ring_w.step(s, n)
+        if s == 0:
+            for n in range(2):
+                ring_kv.begin(n)
         if s < Y // 2:
-            ring_u.step(s)
             relay(ring_u.block(0, s + 1), ubuf.at[ring_u.block(0, s + 1)], 2 * s + 1)
             if s < Y // 2 - 1:
                 relay(ring_u.block(1, s + 1), ubuf.at[ring_u.block(1, s + 1)], 2 * s + 2)
-        if s < Z // 2:
-            ring_w.step(s)
-        if s == 0:
-            ring_kv.begin()
-        if s >= 2:
-            ring_kv.step(kv_next)
-            kv_next += 1
+        if s in KV_STEPS:
+            for n in range(2):
+                ring_kv.step(KV_STEPS.index(s), n)
 
     for b in range(Z):
         row = gid[pl.ds(x * Z + b, 1), :].astype(F32)
@@ -194,6 +202,9 @@
         copy = shared(n, kk)
         copy.start()
         pending.append(copy)
+    if len(KV_STEPS) < Z // 2:
+        for n in range(2):
+            ring_kv.step(len(KV_STEPS), n)
     for n, kk in enumerate(order):
         shared(n, kk).wait_recv()
         total = None
@@ -211,17 +222,9 @@
             acc[...] = total
             dsend[...] = total.astype(BF16)
     exchange(lambda t: dsend.at[t], drecv, ds, dr_)
-    while kv_next < Z // 2 - 1:
-        ring_kv.step(kv_next)
-        kv_next += 1
-    total = acc[x]
-    for d in range(1, X):
-        arrive(drecv, ds, dr_, d)
-        total = total + drecv[x_src[d]].astype(F32)
-    dobuf[x] = total.astype(BF16)
-    exchange(lambda _: dobuf.at[x], dobuf, os_, or_)
-    if kv_next < Z // 2:
-        ring_kv.step(kv_next)
+    for t in range(len(KV_STEPS) + 1, Z // 2):
+        for n in range(2):
+            ring_kv.step(t, n)
     for d in range(1, X):
         arrive(qbuf, qs, qr, d)
 
@@ -261,6 +264,12 @@
     l_own = [jnp.sum(s, axis=0, keepdims=True) for s in sums]
     ml_send[...] = jnp.concatenate([*m_own, *l_own, jnp.zeros((4, Q), F32)], axis=0)
     exchange(lambda _: ml_send, ml_recv, ms, mr)
+    total = acc[x]
+    for d in range(1, X):
+        arrive(drecv, ds, dr_, d)
+        total = total + drecv[x_src[d]].astype(F32)
+    dobuf[x] = total.astype(BF16)
+    exchange(lambda _: dobuf.at[x], dobuf, os_, or_)
     stats = [ml_send[...]]
     for d in range(1, X):
         arrive(ml_recv, ms, mr, d)
@@ -374,6 +383,15 @@
             copy().wait_send()
 
 
+def deliver(*refs):
+    sems = refs[6]
+    copies = [pltpu.make_async_copy(refs[n], refs[n + 3], sems.at[n]) for n in range(3)]
+    for copy in copies:
+        copy.start()
+    for copy in copies:
+        copy.wait()
+
+
 def body(X, Z, Y, queries, key_rows, value_rows, upstream, out_weight, group_ids):
     R, C = queries.shape
     U = upstream.shape[1]
@@ -381,11 +399,13 @@
     K2 = Y // X
     Q = X * R
     groups = group_ids.reshape(X * Z, R)
-    vmem = pl.BlockSpec(memory_space=pltpu.VMEM)
+    vm = pl.BlockSpec(memory_space=pltpu.VMEM)
+    hbm = pl.BlockSpec(memory_space=pl.ANY)
     dma = pltpu.SemaphoreType.DMA
     V = pltpu.VMEM
     out = jax.ShapeDtypeStruct((R, C), BF16)
     scratch = [
+        V((X * Z, R), jnp.int32),
         V((Y, R, U), BF16), V((K2, 2, X, R, U), BF16), V((Z, W, C), BF16), V((X, R, C), BF16),
         V((Z, R, C), BF16), V((Z, R, C), BF16), V((X, R, C), F32), V((X, R, C), BF16),
         V((X, R, C), BF16), V((X, R, C), BF16),
@@ -394,23 +414,32 @@
         V((Z, 2, R, HDIM), F32), V((Z, 2, R, HDIM), F32),
         V((X, R, C), BF16), V((X, R, C), BF16), V((2, HDIM, Q), F32),
         V((2, 2, Z // 2, 2, R, HDIM), BF16), V((2, 2, Z // 2, 2, R, HDIM), BF16),
-        dma((2, Y // 2, 2)), dma((2, Y // 2, 2)), dma((2, Z // 2, 2)), dma((2, Z // 2, 2)),
+        dma((2, Y // 2, NU)), dma((2, Y // 2, NU)), dma((2, Z // 2, NW)), dma((2, Z // 2, NW)),
         dma((2, Z // 2, 2)), dma((2, Z // 2, 2)), dma((X,)), dma((X,)), dma((Y,)), dma((X, K2)),
         dma((K2,)), dma((K2,)),
         dma((X,)), dma((X,)), dma((X,)), dma((X,)), dma((X,)), dma((X,)), dma((X,)), dma((X,)),
-        dma((X,)), dma((X,)), dma((2, 2, Z // 2)), dma((2, 2, Z // 2)),
+        dma((X,)), dma((X,)), dma((2, 2, Z // 2)), dma((2, 2, Z // 2)), dma((6,)),
     ]
-    return pl.pallas_call(
+    grads = pl.pallas_call(
         functools.partial(kernel, X, Z, Y),
         out_shape=(out, out, out),
-        in_specs=[vmem] * 6,
-        out_specs=(vmem, vmem, vmem),
+        in_specs=[hbm] * 6,
+        out_specs=(vm, vm, vm),
         scratch_shapes=scratch,
         name="attention_backward",
         compiler_params=pltpu.CompilerParams(
-            collective_id=0, has_side_effects=True, vmem_limit_bytes=48 * 2**20
+            collective_id=0, has_side_effects=True, vmem_limit_bytes=48*2**20
         ),
-    )(groups, queries, key_rows, value_rows, upstream, out_weight)
+    )(*[pltpu.with_memory_space_constraint(a, pltpu.HBM) for a in (groups, queries, key_rows, value_rows, upstream, out_weight)])
+    return pl.pallas_call(
+        deliver,
+        out_shape=(out, out, out),
+        in_specs=[vm] * 3,
+        out_specs=(hbm, hbm, hbm),
+        scratch_shapes=[dma((3,))],
+        name="deliver",
+        compiler_params=pltpu.CompilerParams(vmem_limit_bytes=32*2**20),
+    )(*grads)
 
 
 def solution(mesh):

time: 77.5 us -> 71.7 us (0.925)
  local copies, waits for them, and re-layouts: 6.9 us -> 0 us
  Pallas kernels: 69.6 us -> 71 us
    unnamed x15 -> x0, local copies, waits for them, and re-layouts: 6.9 us -> none
where the time goes in v2:
time: 71.7 us; the launch traced here: 71.6 us
  Pallas kernels  71 us (99%)
    pallas_call x1, Pallas kernels, body(): pl.pallas_call(functools.partial(kernel, X, Z, Y), out_shape=(out, out, o...  70.3 us

profile of v2, /device:TPU:24, one launch (start us, length us, event | category | flops | bytes accessed | tf_op | source)
XLA Modules:
  0.0 71.6 jit_solution(16452872423624554054)
XLA Ops:
  0.6 70.3 %attention_backward.1 = (bf16[128,256]{1,0:T(8,128)(2,1)S(1)}, bf16[128,256]{1,0:T(8,128)(2,1)S(1)}, bf16[128,256]{1,0:T(8,128)(2,1)S(1)}) custom-call(s32[32,128]{1,0:T(8,128)} %bitcast.1, bf16[128,256]{1,0:T(8,128)(2,1)} %q.1, bf16[128,256]{1,0:T(8,128)(2,1)} %k.1, bf16[128,256]{1,0:T(8,128)(2,1)} %v.1, bf16[128,384]{1,0:T(8,128)(2,1)} %up.1, ...), custom_call_target="tpu_custom_call" | custom-call | tf_op jit(solution)/shard_map/attention_backward/pallas_call | solution.py:423
  70.9 0.7 deliver.1

commit v3 on v2

v3 whole, which is shorter than its diff:
```python
import functools

import jax
import jax.numpy as jnp
from jax import lax
from jax.experimental import pallas as pl
from jax.experimental.pallas import tpu as pltpu
from jax.sharding import PartitionSpec as P

MESH = pl.DeviceIdType.MESH
HDIM = 128
LOG2E = 1.4426950408889634
MASKED = -1e30
FLOOR = -1e29
FIRST = ("w0", "k0", "w1", "k1", "w2", "k2", "w3")
SECOND = (("k3",), ())
THIRD = ()
AHEAD = 1
UNROLL = 8
NW = 2
FAR = (0, 1, 7, 2, 6, 3, 5, 4)
F32 = jnp.float32
BF16 = jnp.bfloat16


def kernel(
    X, Z, Y,
    gid_in, q, k, v, up, w,
    dq_out, dk_out, dv_out,
    gid,
    ubuf, upx, wbuf, qbuf, kbuf, vbuf, acc, dsend, drecv, dobuf,
    ml_send, ml_recv, u_send, u_recv, kid, kt, p_s, dp_s, kpart, vpart,
    dqsend, dqrecv, rsend, rrecv,
    ws, wr, kvs, kvr, qs, qr, xs, xr, sbs, sbr,
    ds, dr_, os_, or_, ms, mr, es, er, gs, gr, rs, rr, ls,
):
    K2 = Y // X
    WB = X * Z // (2 * Y)
    R = q.shape[0]
    Q = X * R
    i, j = lax.axis_index("ctx"), lax.axis_index("head")
    x, z = lax.div(i, Z), lax.rem(i, Z)
    y, c = lax.div(j, 2), lax.rem(j, 2)

    def dev(xx, zz, yy, cc):
        return (xx * Z + zz, yy * 2 + cc)

    def add(a, b, n):
        return lax.rem(a + b + n, n)

    def remote(src, dst, s_sem, r_sem, device):
        return pltpu.make_async_remote_copy(
            src_ref=src, dst_ref=dst, send_sem=s_sem, recv_sem=r_sem,
            device_id=device, device_id_type=MESH,
        )

    z_dev = (dev(x, add(z, 1, Z), y, c), dev(x, add(z, -1, Z), y, c))
    xt, yk = lax.div(y, K2), lax.rem(y, K2)
    away = add(xt, -x, X)
    x_dev = [None] + [dev(add(x, d, X), z, y, c) for d in range(1, X)]
    x_src = [add(x, -d, X) for d in range(X)]
    sibling = dev(x, z, y, 1 - c)

    loads = [
        pltpu.make_async_copy(src, dst, ls.at[n])
        for n, (src, dst) in enumerate([
            (up, ubuf), (w, wbuf.at[z]), (k, kbuf.at[z]), (v, vbuf.at[z]),
            (q, qbuf.at[x]), (gid_in, gid),
        ])
    ]
    for load in loads:
        load.start()

    barrier = pltpu.get_barrier_semaphore()
    peers = [*z_dev, *x_dev[1:], sibling]
    for peer in peers:
        pl.semaphore_signal(barrier, inc=1, device_id=peer, device_id_type=MESH)
    for d in range(X):
        for kk in range(K2):

            @pl.when((d != 0) | (yk != kk) | (away != 0))
            def _():
                source = dev(add(x, d, X), z, K2 * x + kk, c)
                pl.semaphore_signal(barrier, inc=1, device_id=source, device_id_type=MESH)

    pl.semaphore_wait(barrier, len(peers) + X * K2 - jnp.where(away == 0, 1, 0))
    for load in loads:
        load.wait()

    pending = []

    class Ring:
        def __init__(self, n, me, devs, nc, buf, s_sem, r_sem):
            self.n, self.me, self.devs = n, me, devs
            self.buf, self.s, self.r = buf, s_sem, r_sem
            self.last, self.nc = n // 2 - 1, nc

        def chunks(self, d, s):
            order = list(range(self.nc)) if d == 0 else list(range(self.nc))[::-1]
            return order[: self.nc // 2] if s == self.last else order

        def block(self, d, s):
            return add(self.me, -s if d == 0 else s, self.n)

        def send(self, d, s, h):
            b = self.block(d, s)
            copy = remote(
                self.buf(b, h), self.buf(b, h), self.s.at[d, s, h], self.r.at[d, s, h], self.devs[d]
            )
            copy.start()
            pending.append(copy)

        def begin(self, n):
            for d in range(2):
                if n < len(self.chunks(d, 0)):
                    self.send(d, 0, self.chunks(d, 0)[n])

        def step(self, s, n):
            for d in range(2):
                if n < len(self.chunks(d, s)):
                    h = self.chunks(d, s)[n]
                    b = self.block(d, s + 1)
                    remote(
                        self.buf(b, h), self.buf(b, h), self.s.at[d, s, h],
                        self.r.at[d, s, h], self.devs[d],
                    ).wait_recv()
                    if s < self.last and h in self.chunks(d, s + 1):
                        self.send(d, s + 1, h)

    wh = w.shape[0] // NW
    ring_w = Ring(
        Z, z, z_dev, NW,
        lambda b, h: wbuf.at[b, pl.ds(h * wh, wh)],
        ws, wr,
    )
    ring_kv = Ring(
        Z, z, z_dev, 2,
        lambda b, h: (kbuf, vbuf)[h].at[b],
        kvs, kvr,
    )

    scattered = []

    def scatter(step):
        place = upx.at[yk, c, x]
        arrived = xr.at[away, yk]

        def copy():
            return remote(ubuf, place, xs.at[step], arrived, dev(xt, z, add(y, step, Y), c))

        if step > 0:
            copy().start()
            pending.append(copy())
        else:

            @pl.when(away != 0)
            def _():
                copy().start()

            @pl.when(away == 0)
            def _():
                pltpu.make_async_copy(ubuf, place, arrived).start()

            scattered.append((away, copy))

    def exchange(src, dst, s_sem, r_sem, pre=()):
        for d in range(1, X):
            copy = remote(
                src(add(x, d, X)), dst.at[(*pre, x)], s_sem.at[(*pre, d)], r_sem.at[(*pre, d)], x_dev[d]
            )
            copy.start()
            pending.append(copy)

    def arrive(dst, s_sem, r_sem, d, pre=()):
        ref = dst.at[(*pre, x_src[d])]
        remote(ref, ref, s_sem.at[(*pre, d)], r_sem.at[(*pre, d)], x_dev[d]).wait_recv()

    for step in FAR:
        scatter(step)
    for n in range(NW):
        ring_w.begin(n)
    for n in range(2):
        ring_kv.begin(n)
    exchange(lambda _: qbuf.at[x], qbuf, qs, qr)

    def run(steps):
        for step in steps:
            kind, s = step[0], int(step[1])
            if kind == "w" and s < Z // 2:
                for n in range(NW):
                    ring_w.step(s, n)
            if kind == "k" and s < Z // 2:
                for n in range(2):
                    ring_kv.step(s, n)

    run(FIRST)

    for b in range(Z):
        row = gid[pl.ds(x * Z + b, 1), :].astype(F32)
        kid[b] = jnp.broadcast_to(row, (R, R)).T
    qid = jnp.concatenate([gid[pl.ds(b * Z + z, 1), :].astype(F32) for b in range(X)], axis=1)

    turn = lax.rem(y - K2 * x + Y * K2, Y)
    near = jnp.where((turn >= 1) & (turn <= Y // 2), 1, 0) if K2 > 1 else 0
    order = [near, 1 - near] if K2 == 2 else list(range(K2))

    def shared(n, kk, d):
        piece = upx.at[kk, c, x_src[d]]
        return remote(piece, piece, sbs.at[n, d], sbr.at[n, d], sibling)

    turns = sorted(range(X), key=lambda d: min(d, X - d))
    for n, kk in enumerate(order):
        for d in turns:
            dst = upx.at[kk, c, x_src[d]]
            remote(dst, dst, xs.at[0], xr.at[d, kk], sibling).wait_recv()
            copy = shared(n, kk, d)
            copy.start()
            pending.append(copy)
        run(SECOND[n])
    cols = [slice(h * HDIM, (h + 1) * HDIM) for h in range(2)]
    for n, kk in enumerate(order):
        for d in turns:
            piece = upx.at[kk, 1 - c, x_src[d]]
            remote(piece, piece, sbs.at[n, d], sbr.at[n, d], sibling).wait_recv()
        total = None
        for cc in range(2):
            rows = upx[kk, cc].reshape(Q, upx.shape[4])
            weights = wbuf[pl.ds((kk * 2 + cc) * WB, WB)].reshape(upx.shape[4], w.shape[1])
            part = jnp.dot(rows, weights, preferred_element_type=F32)
            total = part if total is None else total + part
        total = total.reshape(X, R, 2 * HDIM)
        for h in range(2):
            value = total[:, :, cols[h]]
            if n > 0:
                value = value + acc[h]
            acc[h] = value
            if n == K2 - 1:
                dsend[h] = value.astype(BF16)
    for h in range(2):
        exchange(lambda t: dsend.at[h, t], drecv, ds, dr_, (h,))
    run(THIRD)
    for d in range(1, X):
        arrive(qbuf, qs, qr, d)

    NT = (((1,), (1,)), ((), ()))
    scale = HDIM ** (-0.5)

    def fold(block, op):
        return op(block.reshape(R // 8, 8, Q), axis=0)

    def loop_scores(b, maxima):
        allowed = jnp.tile(kid[b], (1, X)) <= qid
        out = []
        for h in range(2):
            queries = qbuf[:, :, cols[h]].reshape(Q, HDIM)
            s = lax.dot_general(kbuf[b, :, cols[h]], queries, NT, preferred_element_type=F32)
            s = jnp.where(allowed, s * (scale * LOG2E), MASKED)
            p_s[h, b] = s
            kt[b, cols[h], :] = kbuf[b, :, cols[h]].T
            out.append(jnp.maximum(maxima[h], fold(s, jnp.max)))
        return tuple(out)

    start = jnp.full((8, Q), FLOOR, F32)
    maxima = lax.fori_loop(0, Z, loop_scores, (start, start), unroll=UNROLL)
    m_own = [jnp.max(m, axis=0, keepdims=True) for m in maxima]

    def loop_exp(b, sums):
        out = []
        for h in range(2):
            e = jnp.exp2(p_s[h, b] - m_own[h])
            p_s[h, b] = e
            out.append(sums[h] + fold(e, jnp.sum))
        return tuple(out)

    zero = jnp.zeros((8, Q), F32)
    sums = lax.fori_loop(0, Z, loop_exp, (zero, zero), unroll=UNROLL)
    l_own = [jnp.sum(s, axis=0, keepdims=True) for s in sums]
    ml_send[...] = jnp.concatenate([*m_own, *l_own, jnp.zeros((4, Q), F32)], axis=0)
    exchange(lambda _: ml_send, ml_recv, ms, mr)
    for h in range(2):
        total = acc[h, x]
        for d in turns[1:]:
            arrive(drecv, ds, dr_, d, (h,))
            total = total + drecv[h, x_src[d]].astype(F32)
        dobuf[h, x] = total.astype(BF16)
        exchange(lambda _: dobuf.at[h, x], dobuf, os_, or_, (h,))
    stats = [ml_send[...]]
    for d in range(1, X):
        arrive(ml_recv, ms, mr, d)
        stats.append(ml_recv[x_src[d]])
    factor = []
    for h in range(2):
        m_all = functools.reduce(jnp.maximum, [s[h : h + 1] for s in stats])
        l_all = sum(s[2 + h : 3 + h] * jnp.exp2(s[h : h + 1] - m_all) for s in stats)
        factor.append(jnp.exp2(m_own[h] - m_all) / l_all)

    half = Z // 2
    parts = (vpart, kpart)
    factors = (1.0, scale)

    def rs_first(d, h):
        return 0 if h == d else 1

    def rs_copy(a, d, t, h):
        at = (a, d, t, h)
        return remote(rsend.at[at], rrecv.at[at], rs.at[at], rr.at[at], z_dev[d])

    def rs_step(a, d, h, stage):
        t = rs_first(d, h) + stage
        if t >= half:
            return
        target = add(z, (half - t) if d == 0 else (t - half), Z)
        value = parts[a][target, h] * factors[a]
        if stage > 0:
            rs_copy(a, d, t - 1, h).wait_recv()
            value = value + rrecv[a, d, t - 1, h].astype(F32)
        rsend[a, d, t, h] = value.astype(BF16)
        copy = rs_copy(a, d, t, h)
        copy.start()
        pending.append(copy)

    def rs_end(a, out):
        for h in range(2):
            value = parts[a][z, h] * factors[a]
            for d in range(2):
                if rs_first(d, h) < half:
                    rs_copy(a, d, half - 1, h).wait_recv()
                    value = value + rrecv[a, d, half - 1, h].astype(F32)
            out[:, cols[h]] = value.astype(BF16)

    def rs_stage(a, stage):
        for n in range(2):
            for d in range(2):
                rs_step(a, d, (d, 1 - d)[n], stage)

    for h in range(2):
        for d in turns[1:]:
            arrive(dobuf, os_, or_, d, (h,))

        def loop_probs(b, total):
            grads = dobuf[h].reshape(Q, HDIM)
            g = lax.dot_general(vbuf[b, :, cols[h]], grads, NT, preferred_element_type=F32)
            prob = p_s[h, b] * factor[h]
            p_s[h, b] = prob
            dp_s[h, b] = g
            vpart[b, h] = jnp.dot(prob.astype(BF16), grads, preferred_element_type=F32)
            return total + fold(prob * g, jnp.sum)

        total = lax.fori_loop(0, Z, loop_probs, zero, unroll=UNROLL)
        u_send[h] = total
        exchange(lambda _: u_send.at[h], u_recv, es, er, (h,))
        for d in range(2):
            rs_step(0, d, h, 0)
    for stage in range(1, AHEAD):
        rs_stage(0, stage)

    for h in range(2):
        total = u_send[h]
        for d in turns[1:]:
            arrive(u_recv, es, er, d, (h,))
            total = total + u_recv[h, x_src[d]]
        delta = jnp.sum(total, axis=0, keepdims=True)

        def loop_grads(b, total):
            g = (p_s[h, b] * (dp_s[h, b] - delta)).astype(BF16)
            queries = qbuf[:, :, cols[h]].reshape(Q, HDIM)
            kpart[b, h] = jnp.dot(g, queries, preferred_element_type=F32)
            return total + jnp.dot(kt[b, cols[h], :], g, preferred_element_type=F32)

        dq = lax.fori_loop(0, Z, loop_grads, jnp.zeros((HDIM, Q), F32), unroll=UNROLL)
        for d in range(2):
            rs_step(1, d, h, 0)
        for b in range(X):
            part = dq[:, b * R : (b + 1) * R].T * scale
            acc[h, b] = part
            dqsend[h, b] = part.astype(BF16)
        exchange(lambda t: dqsend.at[h, t], dqrecv, gs, gr, (h,))
    for stage in range(1, half):
        if stage + AHEAD - 1 < half:
            rs_stage(0, stage + AHEAD - 1)
        rs_stage(1, stage)
    for h in range(2):
        total = acc[h, x]
        for d in turns[1:]:
            arrive(dqrecv, gs, gr, d, (h,))
            total = total + dqrecv[h, x_src[d]].astype(F32)
        dq_out[:, cols[h]] = total.astype(BF16)
    rs_end(0, dv_out)
    rs_end(1, dk_out)

    for copy in pending:
        copy.wait_send()
    for d, copy in scattered:

        @pl.when(d != 0)
        def _():
            copy().wait_send()


def deliver(*refs):
    sems = refs[6]
    copies = [pltpu.make_async_copy(refs[n], refs[n + 3], sems.at[n]) for n in range(3)]
    for copy in copies:
        copy.start()
    for copy in copies:
        copy.wait()


def body(X, Z, Y, queries, key_rows, value_rows, upstream, out_weight, group_ids):
    R, C = queries.shape
    U = upstream.shape[1]
    W = out_weight.shape[0]
    K2 = Y // X
    Q = X * R
    groups = group_ids.reshape(X * Z, R)
    vm = pl.BlockSpec(memory_space=pltpu.VMEM)
    hbm = pl.BlockSpec(memory_space=pl.ANY)
    dma = pltpu.SemaphoreType.DMA
    V = pltpu.VMEM
    out = jax.ShapeDtypeStruct((R, C), BF16)
    scratch = [
        V((X * Z, R), jnp.int32),
        V((R, U), BF16), V((K2, 2, X, R, U), BF16), V((Z, W, C), BF16), V((X, R, C), BF16),
        V((Z, R, C), BF16), V((Z, R, C), BF16), V((2, X, R, HDIM), F32), V((2, X, R, HDIM), BF16),
        V((2, X, R, HDIM), BF16), V((2, X, R, HDIM), BF16),
        V((8, Q), F32), V((X, 8, Q), F32), V((2, 8, Q), F32), V((2, X, 8, Q), F32),
        V((Z, R, R), F32), V((Z, C, R), BF16), V((2, Z, R, Q), F32), V((2, Z, R, Q), F32),
        V((Z, 2, R, HDIM), F32), V((Z, 2, R, HDIM), F32),
        V((2, X, R, HDIM), BF16), V((2, X, R, HDIM), BF16),
        V((2, 2, Z // 2, 2, R, HDIM), BF16), V((2, 2, Z // 2, 2, R, HDIM), BF16),
        dma((2, Z // 2, NW)), dma((2, Z // 2, NW)),
        dma((2, Z // 2, 2)), dma((2, Z // 2, 2)), dma((X,)), dma((X,)), dma((Y,)), dma((X, K2)),
        dma((K2, X)), dma((K2, X)),
        dma((2, X)), dma((2, X)), dma((2, X)), dma((2, X)), dma((X,)), dma((X,)), dma((2, X)), dma((2, X)),
        dma((2, X)), dma((2, X)), dma((2, 2, Z // 2, 2)), dma((2, 2, Z // 2, 2)), dma((6,)),
    ]
    grads = pl.pallas_call(
        functools.partial(kernel, X, Z, Y),
        out_shape=(out, out, out),
        in_specs=[hbm] * 6,
        out_specs=(vm, vm, vm),
        scratch_shapes=scratch,
        name="attention_backward",
        compiler_params=pltpu.CompilerParams(
            collective_id=0, has_side_effects=True, vmem_limit_bytes=48*2**20
        ),
    )(*[pltpu.with_memory_space_constraint(a, pltpu.HBM) for a in (groups, queries, key_rows, value_rows, upstream, out_weight)])
    return pl.pallas_call(
        deliver,
        out_shape=(out, out, out),
        in_specs=[vm] * 3,
        out_specs=(hbm, hbm, hbm),
        scratch_shapes=[dma((3,))],
        name="deliver",
        compiler_params=pltpu.CompilerParams(vmem_limit_bytes=32*2**20),
    )(*grads)


def solution(mesh):
    split = P("ctx", "head")
    X, Z, Y = 4, mesh.shape["ctx"] // 4, mesh.shape["head"] // 2
    return jax.shard_map(
        functools.partial(body, X, Z, Y),
        mesh=mesh,
        in_specs=(split, split, split, split, split, P()),
        out_specs=(split, split, split),
        check_vma=False,
    )
```

time: 71.7 us -> 68 us (0.948)
  the two profiles are of different devices: /device:TPU:24 before, /device:TPU:16 now
where the time goes in v3:
time: 68 us; the launch traced here: 67.9 us
  Pallas kernels  67.2 us (99%)
    pallas_call x1, Pallas kernels, body(): pl.pallas_call(functools.partial(kernel, X, Z, Y), out_shape=(out, out, o...  66.5 us

profile of v3, /device:TPU:16, one launch (start us, length us, event | category | flops | bytes accessed | tf_op | source)
XLA Modules:
  0.0 67.9 jit_solution(17898694666019116344)
XLA Ops:
  0.6 66.5 %attention_backward.1 = (bf16[128,256]{1,0:T(8,128)(2,1)S(1)}, bf16[128,256]{1,0:T(8,128)(2,1)S(1)}, bf16[128,256]{1,0:T(8,128)(2,1)S(1)}) custom-call(s32[32,128]{1,0:T(8,128)} %bitcast.1, bf16[128,256]{1,0:T(8,128)(2,1)} %q.1, bf16[128,256]{1,0:T(8,128)(2,1)} %k.1, bf16[128,256]{1,0:T(8,128)(2,1)} %v.1, bf16[128,384]{1,0:T(8,128)(2,1)} %up.1, ...), custom_call_target="tpu_custom_call" | custom-call | tf_op jit(solution)/shard_map/attention_backward/pallas_call | solution.py:437
  67.2 0.7 %deliver.1 = (bf16[128,256]{1,0:T(8,128)(2,1)}, bf16[128,256]{1,0:T(8,128)(2,1)}, bf16[128,256]{1,0:T(8,128)(2,1)}) custom-call(bf16[128,256]{1,0:T(8,128)(2,1)S(1)} %get-tuple-element.6.refs_0_, bf16[128,256]{1,0:T(8,128)(2,1)S(1)} %get-tuple-element.7.refs_1_, bf16[128,256]{1,0:T(8,128)(2,1)S(1)} %get-tuple-element.8.refs_2_), custom_call_target="tpu_custom_call" | custom-call | tf_op jit(solution)/shard_map/deliver/pallas_call | solution.py:448

commit v4 on v3

--- a/solution.py
+++ b/solution.py
@@ -175,10 +175,10 @@
         ref = dst.at[(*pre, x_src[d])]
         remote(ref, ref, s_sem.at[(*pre, d)], r_sem.at[(*pre, d)], x_dev[d]).wait_recv()
 
+    for n in range(NW):
+        ring_w.begin(n)
     for step in FAR:
         scatter(step)
-    for n in range(NW):
-        ring_w.begin(n)
     for n in range(2):
         ring_kv.begin(n)
     exchange(lambda _: qbuf.at[x], qbuf, qs, qr)

time: 68 us -> 68 us (level)
  no operation moved by 1% of the time
where the time goes in v4:
time: 68 us; the launch traced here: 67.9 us
  Pallas kernels  67.2 us (99%)
    pallas_call x1, Pallas kernels, body(): pl.pallas_call(functools.partial(kernel, X, Z, Y), out_shape=(out, out, o...  66.5 us

profile of v4, /device:TPU:16, one launch (start us, length us, event | category | flops | bytes accessed | tf_op | source)
XLA Modules:
  0.0 67.9 jit_solution(12799467088374936370)
XLA Ops:
  0.6 66.5 %attention_backward.1 = (bf16[128,256]{1,0:T(8,128)(2,1)S(1)}, bf16[128,256]{1,0:T(8,128)(2,1)S(1)}, bf16[128,256]{1,0:T(8,128)(2,1)S(1)}) custom-call(s32[32,128]{1,0:T(8,128)} %bitcast.1, bf16[128,256]{1,0:T(8,128)(2,1)} %q.1, bf16[128,256]{1,0:T(8,128)(2,1)} %k.1, bf16[128,256]{1,0:T(8,128)(2,1)} %v.1, bf16[128,384]{1,0:T(8,128)(2,1)} %up.1, ...), custom_call_target="tpu_custom_call" | custom-call | tf_op jit(solution)/shard_map/attention_backward/pallas_call | solution.py:437
  67.2 0.7 %deliver.1 = (bf16[128,256]{1,0:T(8,128)(2,1)}, bf16[128,256]{1,0:T(8,128)(2,1)}, bf16[128,256]{1,0:T(8,128)(2,1)}) custom-call(bf16[128,256]{1,0:T(8,128)(2,1)S(1)} %get-tuple-element.6.refs_0_, bf16[128,256]{1,0:T(8,128)(2,1)S(1)} %get-tuple-element.7.refs_1_, bf16[128,256]{1,0:T(8,128)(2,1)S(1)} %get-tuple-element.8.refs_2_), custom_call_target="tpu_custom_call" | custom-call | tf_op jit(solution)/shard_map/deliver/pallas_call | solution.py:448
